TPU v7x, 32 devices: a whole 2x2x4 slice. The times are simulated.
32 devices in a mesh: grp: 2 (over x), tx: 8 (over z, y), ty: 2 (over core).
Axes of the slice: x: 2, y: 2, z: 4, core: 2. Of those that a mesh axis runs over, the one named last changes fastest.
Arguments:
- raster: bfloat16 [128, 16, 128, 128], P(('grp', 'tx'), 'ty'), parts along dimension 0, may hold values from 0 to 1
- kernels: bfloat16 [128, 4096], replicated, may hold values from -0.5 to 0.5
- kernel_weights: float32 [16], replicated, may hold values from 0.05 to 1
- cut_weights: float32 [128], replicated, may hold values from -0.3 to 0.3
- need_list: int32 [16, 2, 84], P(('grp', 'tx'), 'ty'), parts along dimension 0, may hold values from 0 to 99, as said below
- point_slot: int32 [16, 2, 3072], P(('grp', 'tx'), 'ty'), parts along dimension 0, may hold values from 0 to 83, as said below
- point_row: int32 [16, 2, 3072], P(('grp', 'tx'), 'ty'), parts along dimension 0, may hold values from 0 to 127
- threshold: float32 [16, 2, 3072], P(('grp', 'tx'), 'ty'), parts along dimension 0, may hold values from -2 to 2
- point_weight: float32 [16, 2, 3072], P(('grp', 'tx'), 'ty'), parts along dimension 0, may hold values from 1 to 48
- jac_ids: int32 [16, 2, 24, 4], P(('grp', 'tx'), 'ty'), parts along dimension 0, may hold values from 0 to 59
- jacobian: float32 [16, 2, 24, 4, 128, 128], P(('grp', 'tx'), 'ty'), parts along dimension 0, may hold values from -0.25 to 0.25
Outputs:
- epe: float32 [16, 2, 3072], P(('grp', 'tx'), 'ty'), parts along dimension 0
- step: float32 [16, 2, 1536], P(('grp', 'tx'), 'ty'), parts along dimension 0
There are 2 independent parts, one for each index of `grp`. A program takes and returns all parts, laid end to end along the dimension named above; an argument that names none is the same for every part. Nothing has to cross between parts.
Inputs may be any that keep to these rules, and one draw needn't show every extreme that they name: `need_list`: each tile's list names 84 distinct blocks of its extended grid: all 64 blocks it owns and 20 of the cycle around them. `point_slot`: each need-list entry that names a cycle block is named by exactly 16 cut lines of the tile; all other cut lines name owned blocks.
All inputs are finite; a program needn't handle non-finite values.
Results may differ from a plain program's by a relative error of at most 0.0003.
Values may be sent and summed in bfloat16 or wider, within the bound.
A program may use at most 64 MiB of HBM per device.

v0:
```python
import math

import jax
import jax.numpy as jnp
from jax import lax
from jax.sharding import PartitionSpec as P

BS = 128
NK = 16
NEED = 84
P_SIZE = 3072
SEG = 1536
NNZ = 4
ITERS = 3


damping = 1.0


def extended_2(block, sides, width):
    for axis, dim in sides:
        count = lax.axis_size(axis)
        forward = [(i, i + 1) for i in range(count - 1)]
        backward = [(target, source) for source, target in forward]
        low = lax.ppermute(
            lax.slice_in_dim(block, block.shape[dim] - width, None, axis=dim), axis, forward
        )
        high = lax.ppermute(lax.slice_in_dim(block, 0, width, axis=dim), axis, backward)
        block = jnp.concatenate([low, block, high], axis=dim)
    return block


def on_device(
    raster,
    kernels,
    kernel_weights,
    cut_weights,
    need_list,
    point_slot,
    point_row,
    threshold,
    point_weight,
    jac_ids,
    jacobian,
):
    seg_blocks = SEG // BS
    pt_blocks = P_SIZE // BS
    need_ids = need_list.reshape(NEED)
    slots = point_slot.reshape(P_SIZE)
    rows_in = point_row.reshape(P_SIZE)
    matches = slots[:, None] == jnp.arange(NEED, dtype=jnp.int32)[None, :]
    blocks = jnp.sum(jnp.where(matches, need_ids[None, :], 0), axis=1)
    extended = extended_2(raster, (("tx", 0), ("ty", 1)), 1)
    row_data = extended.reshape(-1, BS)[blocks * BS + rows_in]
    weight_pair = jnp.repeat(kernel_weights, 2)
    span = math.gcd(P_SIZE, 512)

    def evaluate(pieces):
        row_piece, level_piece = pieces
        amplitude = jnp.dot(row_piece, kernels, preferred_element_type=jnp.float32).reshape(
            span, 2 * NK, BS
        )
        intensity = jnp.einsum(
            "pkc,k->pc", amplitude * amplitude, weight_pair, precision=lax.Precision.HIGHEST
        )
        return jnp.dot(intensity, cut_weights, precision=lax.Precision.HIGHEST) - level_piece

    epe = lax.map(
        evaluate,
        (row_data.reshape(P_SIZE // span, span, BS), threshold.reshape(P_SIZE // span, span)),
    ).reshape(P_SIZE)
    jac_blocks = jacobian.reshape(pt_blocks, NNZ, BS, BS)
    flat_ids = jac_ids.reshape(pt_blocks * NNZ)
    selector = (flat_ids[:, None] == jnp.arange(5 * seg_blocks, dtype=jnp.int32)[None, :]).astype(
        jnp.float32
    )
    weights = point_weight.reshape(P_SIZE)

    def forward(vector):
        beside_all = extended_2(vector.reshape(1, 1, SEG), (("tx", 0), ("ty", 1)), 1)
        stacked = jnp.stack(
            [
                beside_all[1, 1],
                beside_all[0, 1],
                beside_all[2, 1],
                beside_all[1, 0],
                beside_all[1, 2],
            ]
        ).reshape(5 * seg_blocks, BS)
        gathered = jnp.dot(selector, stacked, precision=lax.Precision.HIGHEST).reshape(
            pt_blocks, NNZ, BS
        )
        result = jnp.einsum("nkij,nkj->ni", jac_blocks, gathered, precision=lax.Precision.HIGHEST)
        return result.reshape(P_SIZE)

    def backward(values):
        contrib = jnp.einsum(
            "nkij,ni->nkj",
            jac_blocks,
            values.reshape(pt_blocks, BS),
            precision=lax.Precision.HIGHEST,
        )
        contrib = contrib.reshape(pt_blocks * NNZ, BS)
        summed = jnp.dot(selector.T, contrib, precision=lax.Precision.HIGHEST).reshape(5, SEG)
        outgoing = jnp.stack([jnp.stack([summed[1], summed[4]]), jnp.stack([summed[3], summed[2]])])
        arrived = extended_2(outgoing, (("tx", 0), ("ty", 1)), 1)
        return summed[0] + arrived[0, 2] + arrived[3, 1] + arrived[1, 0] + arrived[2, 3]

    def apply_normal(vector):
        return backward(weights * forward(vector)) + damping * vector

    def two_products(residual, image):
        return lax.psum((jnp.sum(residual * residual), jnp.sum(residual * image)), ("tx", "ty"))

    rhs = -backward(weights * epe)
    step = jnp.zeros_like(rhs)
    residual = rhs
    image = apply_normal(residual)
    norm_now, product = two_products(residual, image)
    alpha = norm_now / product
    direction, along = (residual, image)
    for turn in range(ITERS):
        step = step + alpha * direction
        residual = residual - alpha * along
        if turn + 1 < ITERS:
            image = apply_normal(residual)
            norm_next, product = two_products(residual, image)
            ratio = norm_next / norm_now
            alpha = norm_next / (product - ratio * norm_next / alpha)
            direction = residual + ratio * direction
            along = image + ratio * along
            norm_now = norm_next
    return (epe.reshape(1, 1, P_SIZE), step.reshape(1, 1, SEG))


def solution(mesh):
    in_specs = (
        P(("grp", "tx"), "ty", None, None),
        P(),
        P(),
        P(),
        P(("grp", "tx"), "ty", None),
        P(("grp", "tx"), "ty", None),
        P(("grp", "tx"), "ty", None),
        P(("grp", "tx"), "ty", None),
        P(("grp", "tx"), "ty", None),
        P(("grp", "tx"), "ty", None, None),
        P(("grp", "tx"), "ty", None, None, None, None),
    )
    out_specs = (P(("grp", "tx"), "ty", None), P(("grp", "tx"), "ty", None))
    return jax.shard_map(
        on_device, mesh=mesh, in_specs=in_specs, out_specs=out_specs, check_vma=False
    )
```

profile of v0, /device:TPU:0, one launch (start us, length us, event | category | flops | bytes accessed | tf_op | source)
XLA Modules:
  0.0 387.0 jit_solution(10036441451052115744)
XLA Ops:
  1.8 4.9 %collective-permute-start = (bf16[1,8,128,128]{3,2,1,0:T(8,128)(2,1)S(1)}, bf16[1,8,128,128]{3,2,1,0:T(8,128)(2,1)S(1)}, u32[]{:S(2)}, u32[]{:S(2)}) collective-permute-start(bf16[1,8,128,128]{3,2,1,0:T(8,128)(2,1)S(1)} %get-tuple-element.101), channel_id=1, source_target_pairs={{0,2},{2,4},{4,6},{6,8},{8,10},{10,12},{12,14},{1,3},{3,5},{5,7},{... | collective-permute-start | bytes 786440 | tf_op jit(solution)/shard_map/ppermute | solution.py:25
  9.0 8.9 %collective-permute-done = bf16[1,8,128,128]{3,2,1,0:T(8,128)(2,1)S(1)} collective-permute-done((bf16[1,8,128,128]{3,2,1,0:T(8,128)(2,1)S(1)}, bf16[1,8,128,128]{3,2,1,0:T(8,128)(2,1)S(1)}, u32[]{:S(2)}, u32[]{:S(2)}) %collective-permute-start) | collective-permute-done | bytes 262176 | tf_op jit(solution)/shard_map/ppermute | solution.py:25
  30.2 10.7 %gather_fusion = bf16[3072,128]{1,0:T(8,128)(2,1)S(1)} fusion(bf16[12800,128]{1,0:T(8,128)(2,1)} %bitcast.388, s32[3072]{0:T(1024)S(1)} %broadcast_clamp_fusion), kind=kCustom, calls=%fused_computation | custom fusion | bytes 1585152 | tf_op jit(solution)/shard_map/gather | solution.py:54
  40.9 103.9 %while.11 = (s32[]{:T(128)}, f32[6,512]{1,0:T(8,128)S(1)}, bf16[6,512,128]{2,1,0:T(8,128)(2,1)S(1)}, bf16[128,4096]{0,1:T(8,128)(2,1)S(1)}, f32[128]{0:T(128)S(1...) while((s32[]{:T(128)}, f32[6,512]{1,0:T(8,128)S(1)}, ...), condition=%wide.region_2.3_spmd.clone, body=%wide.region_1.2_spmd.clone.sunk | while | flops 564920832 | bytes 18498728 | solution.py:68
  40.9 4.5 %convolution_multiply_fusion.2 = f32[512,32,128]{2,0,1:T(8,128)} fusion(bf16[32,128,128]{2,1,0:T(8,128)(2,1)S(1)} %bitcast.387, bf16[6,512,128]{2,1,0:T(8,128)(2,1)S(1)} %get-tuple-element.204, s32[]{:T(128)} %get-tuple-element.193), kind=kOutput, calls=%fused_computation.4.clone.1 | convolution fusion | flops 538968064 | bytes 9568260 | tf_op jit(solution)/shard_map/while/body/eval_jaxpr/dot_general | solution.py:60
  45.5 12.2 %fusion.106 = f32[1,512,128]{2,0,1:T(1,128)S(1)} fusion(f32[32,1,1]{0,1,2:T(1,128)S(1)} %reshape.496, f32[512,32,128]{2,0,1:T(8,128)} %convolution_multiply_fusion.2), kind=kOutput, calls=%fused_computation.2.clone.1 | convolution fusion | flops 25165824 | bytes 8650880 | tf_op jit(solution)/shard_map/while/body/eval_jaxpr/pkc,k->pc/dot_general | solution.py:63
  58.2 4.5 %convolution_multiply_fusion.2 = f32[512,32,128]{2,0,1:T(8,128)} fusion(bf16[32,128,128]{2,1,0:T(8,128)(2,1)S(1)} %bitcast.387, bf16[6,512,128]{2,1,0:T(8,128)(2,1)S(1)} %get-tuple-element.204, s32[]{:T(128)} %get-tuple-element.193), kind=kOutput, calls=%fused_computation.4.clone.1 | convolution fusion | flops 538968064 | bytes 9568260 | tf_op jit(solution)/shard_map/while/body/eval_jaxpr/dot_general | solution.py:60
  62.8 12.2 %fusion.106 = f32[1,512,128]{2,0,1:T(1,128)S(1)} fusion(f32[32,1,1]{0,1,2:T(1,128)S(1)} %reshape.496, f32[512,32,128]{2,0,1:T(8,128)} %convolution_multiply_fusion.2), kind=kOutput, calls=%fused_computation.2.clone.1 | convolution fusion | flops 25165824 | bytes 8650880 | tf_op jit(solution)/shard_map/while/body/eval_jaxpr/pkc,k->pc/dot_general | solution.py:63
  75.5 4.5 %convolution_multiply_fusion.2 = f32[512,32,128]{2,0,1:T(8,128)} fusion(bf16[32,128,128]{2,1,0:T(8,128)(2,1)S(1)} %bitcast.387, bf16[6,512,128]{2,1,0:T(8,128)(2,1)S(1)} %get-tuple-element.204, s32[]{:T(128)} %get-tuple-element.193), kind=kOutput, calls=%fused_computation.4.clone.1 | convolution fusion | flops 538968064 | bytes 9568260 | tf_op jit(solution)/shard_map/while/body/eval_jaxpr/dot_general | solution.py:60
  80.2 12.2 %fusion.106 = f32[1,512,128]{2,0,1:T(1,128)S(1)} fusion(f32[32,1,1]{0,1,2:T(1,128)S(1)} %reshape.496, f32[512,32,128]{2,0,1:T(8,128)} %convolution_multiply_fusion.2), kind=kOutput, calls=%fused_computation.2.clone.1 | convolution fusion | flops 25165824 | bytes 8650880 | tf_op jit(solution)/shard_map/while/body/eval_jaxpr/pkc,k->pc/dot_general | solution.py:63
  92.8 4.5 %convolution_multiply_fusion.2 = f32[512,32,128]{2,0,1:T(8,128)} fusion(bf16[32,128,128]{2,1,0:T(8,128)(2,1)S(1)} %bitcast.387, bf16[6,512,128]{2,1,0:T(8,128)(2,1)S(1)} %get-tuple-element.204, s32[]{:T(128)} %get-tuple-element.193), kind=kOutput, calls=%fused_computation.4.clone.1 | convolution fusion | flops 538968064 | bytes 9568260 | tf_op jit(solution)/shard_map/while/body/eval_jaxpr/dot_general | solution.py:60
  97.5 12.2 %fusion.106 = f32[1,512,128]{2,0,1:T(1,128)S(1)} fusion(f32[32,1,1]{0,1,2:T(1,128)S(1)} %reshape.496, f32[512,32,128]{2,0,1:T(8,128)} %convolution_multiply_fusion.2), kind=kOutput, calls=%fused_computation.2.clone.1 | convolution fusion | flops 25165824 | bytes 8650880 | tf_op jit(solution)/shard_map/while/body/eval_jaxpr/pkc,k->pc/dot_general | solution.py:63
  114.8 12.2 %fusion.106 = f32[1,512,128]{2,0,1:T(1,128)S(1)} fusion(f32[32,1,1]{0,1,2:T(1,128)S(1)} %reshape.496, f32[512,32,128]{2,0,1:T(8,128)} %convolution_multiply_fusion.2), kind=kOutput, calls=%fused_computation.2.clone.1 | convolution fusion | flops 25165824 | bytes 8650880 | tf_op jit(solution)/shard_map/while/body/eval_jaxpr/pkc,k->pc/dot_general | solution.py:63
  132.1 12.2 %fusion.106 = f32[1,512,128]{2,0,1:T(1,128)S(1)} fusion(f32[32,1,1]{0,1,2:T(1,128)S(1)} %reshape.496, f32[512,32,128]{2,0,1:T(8,128)} %convolution_multiply_fusion.2), kind=kOutput, calls=%fused_computation.2.clone.1 | convolution fusion | flops 25165824 | bytes 8650880 | tf_op jit(solution)/shard_map/while/body/eval_jaxpr/pkc,k->pc/dot_general | solution.py:63
  144.8 5.1 %fusion.21 = f32[24,1,4,128]{3,1,2,0:T(1,128)S(1)} fusion(f32[24,128,1,1]{1,2,3,0:T(1,128)S(1)} %bitcast.404, f32[1,1,24,4,128,128]{5,4,3,2,1,0:T(8,128)} %param.23), kind=kOutput, calls=%fused_computation.23 | convolution fusion | flops 18874368 | bytes 6352896 | tf_op jit(solution)/shard_map/nkij,ni->nkj/dot_general | solution.py:97
  180.0 7.3 %fusion.19 = f32[24,1,128,1]{2,1,3,0:T(1,128)S(1)} fusion(f32[1,1,24,4,128,128]{5,4,3,2,1,0:T(8,128)} %param.23, f32[24,4,128,1]{2,0,1,3:T(8,128)S(1)} %convolution_bitcast_fusion.2), kind=kOutput, calls=%fused_computation.21 | convolution fusion | flops 18874368 | bytes 6352896 | tf_op jit(solution)/shard_map/nkij,nkj->ni/dot_general | solution.py:93
  187.3 5.1 %fusion.17 = f32[24,1,4,128]{3,1,2,0:T(1,128)S(1)} fusion(f32[24,128,1,1]{1,2,3,0:T(1,128)S(1)} %bitcast.406, f32[1,1,24,4,128,128]{5,4,3,2,1,0:T(8,128)} %param.23), kind=kOutput, calls=%fused_computation.19 | convolution fusion | flops 18874368 | bytes 6352896 | tf_op jit(solution)/shard_map/nkij,ni->nkj/dot_general | solution.py:97
  208.5 30.4 %all-reduce.2 = (f32[]{:T(128)}, f32[]{:T(128)}) all-reduce(f32[]{:T(128)} %get-tuple-element.69, f32[]{:T(128)} %get-tuple-element.68), channel_id=1, replica_groups=mesh['grp'=2,'tx'=8,'ty'=2] {'tx','ty'}, use_global_device_ids=true, to_apply=%region_4.5 | all-reduce | flops 2 | bytes 16 | tf_op jit(solution)/shard_map/psum | solution.py:113
  252.6 7.3 %fusion.15 = f32[24,1,128,1]{2,1,3,0:T(1,128)S(1)} fusion(f32[1,1,24,4,128,128]{5,4,3,2,1,0:T(8,128)} %param.23, f32[24,4,128,1]{2,0,1,3:T(8,128)S(1)} %convolution_bitcast_fusion.1), kind=kOutput, calls=%fused_computation.17 | convolution fusion | flops 18874368 | bytes 6352896 | tf_op jit(solution)/shard_map/nkij,nkj->ni/dot_general | solution.py:93
  259.9 5.1 %fusion.13 = f32[24,1,4,128]{3,1,2,0:T(1,128)S(1)} fusion(f32[24,128,1,1]{1,2,3,0:T(1,128)S(1)} %bitcast.408, f32[1,1,24,4,128,128]{5,4,3,2,1,0:T(8,128)} %param.23), kind=kOutput, calls=%fused_computation.15 | convolution fusion | flops 18874368 | bytes 6352896 | tf_op jit(solution)/shard_map/nkij,ni->nkj/dot_general | solution.py:97
  278.6 30.5 %all-reduce.1 = (f32[]{:T(128)}, f32[]{:T(128)}) all-reduce(f32[]{:T(128)} %get-tuple-element.67, f32[]{:T(128)} %get-tuple-element.66), channel_id=1, replica_groups=mesh['grp'=2,'tx'=8,'ty'=2] {'tx','ty'}, use_global_device_ids=true, to_apply=%region_8.9 | all-reduce | flops 2 | bytes 16 | tf_op jit(solution)/shard_map/psum | solution.py:113
  326.2 7.3 %fusion.11 = f32[24,1,128,1]{2,1,3,0:T(1,128)S(1)} fusion(f32[1,1,24,4,128,128]{5,4,3,2,1,0:T(8,128)} %param.23, f32[24,4,128,1]{2,0,1,3:T(8,128)S(1)} %convolution_bitcast_fusion), kind=kOutput, calls=%fused_computation.13 | convolution fusion | flops 18874368 | bytes 6352896 | tf_op jit(solution)/shard_map/nkij,nkj->ni/dot_general | solution.py:93
  333.5 5.1 %fusion.9 = f32[24,1,4,128]{3,1,2,0:T(1,128)S(1)} fusion(f32[24,128,1,1]{1,2,3,0:T(1,128)S(1)} %bitcast.410, f32[1,1,24,4,128,128]{5,4,3,2,1,0:T(8,128)} %param.23), kind=kOutput, calls=%fused_computation.11 | convolution fusion | flops 18874368 | bytes 6352896 | tf_op jit(solution)/shard_map/nkij,ni->nkj/dot_general | solution.py:97
  352.1 30.4 %all-reduce = (f32[]{:T(128)}, f32[]{:T(128)}) all-reduce(f32[]{:T(128)} %get-tuple-element.65, f32[]{:T(128)} %get-tuple-element.64), channel_id=1, replica_groups=mesh['grp'=2,'tx'=8,'ty'=2] {'tx','ty'}, use_global_device_ids=true, to_apply=%region_12.13 | all-reduce | flops 2 | bytes 16 | tf_op jit(solution)/shard_map/psum | solution.py:113
  (220 shorter events, 126.0 us)
Async XLA Ops:
  1.8 16.0 %collective-permute-start = (bf16[1,8,128,128]{3,2,1,0:T(8,128)(2,1)S(1)}, bf16[1,8,128,128]{3,2,1,0:T(8,128)(2,1)S(1)}, u32[]{:S(2)}, u32[]{:S(2)}) collective-permute-start(bf16[1,8,128,128]{3,2,1,0:T(8,128)(2,1)S(1)} %get-tuple-element.101), channel_id=1, source_target_pairs={{0,2},{2,4},{4,6},{6,8},{8,10},{10,12},{12,14},{1,3},{3,5},{5,7},{... | collective-permute-start | bytes 786440 | tf_op jit(solution)/shard_map/ppermute | solution.py:25
  6.7 13.2 %collective-permute-start.1 = (bf16[1,8,128,128]{3,2,1,0:T(8,128)(2,1)S(1)}, bf16[1,8,128,128]{3,2,1,0:T(8,128)(2,1)S(1)}, u32[]{:S(2)}, u32[]{:S(2)}) collective-permute-start(bf16[1,8,128,128]{3,2,1,0:T(8,128)(2,1)S(1)} %get-tuple-element.100), channel_id=1, source_target_pairs={{2,0},{4,2},{6,4},{8,6},{10,8},{12,10},{14,12},{3,1},{5,3},{7,5},{... | collective-permute-start | bytes 786440 | tf_op jit(solution)/shard_map/ppermute | solution.py:28
  21.5 4.8 %collective-permute-start.2 = (bf16[10,1,128,128]{3,2,1,0:T(8,128)(2,1)S(1)}, bf16[10,1,128,128]{3,2,1,0:T(8,128)(2,1)S(1)}, u32[]{:S(2)}, u32[]{:S(2)}) collective-permute-start(bf16[10,1,128,128]{3,2,1,0:T(8,128)(2,1)S(1)} %get-tuple-element.98), channel_id=1, source_target_pairs={{0,1},{2,3},{4,5},{6,7},{8,9},{10,11},{12,13},{14,15},{16,17},{18,... | collective-permute-start | bytes 983048 | tf_op jit(solution)/shard_map/ppermute | solution.py:25
  150.2 5.8 %collective-permute-start.4 = (f32[1,2,1536]{2,1,0:T(2,128)S(1)}, f32[1,2,1536]{2,1,0:T(2,128)S(1)}, u32[]{:S(2)}, u32[]{:S(2)}) collective-permute-start(f32[1,2,1536]{2,1,0:T(2,128)S(1)} %maximum_bitcast_fusion), channel_id=1, source_target_pairs={{0,2},{2,4},{4,6},{6,8},{8,10},{10,12},{12,14},{1,3},{3,5},{5,7},{... | collective-permute-start | bytes 36872 | tf_op jit(solution)/shard_map/ppermute | solution.py:25
  154.7 5.6 %collective-permute-start.5 = (f32[1,2,1536]{2,1,0:T(2,128)S(1)}, f32[1,2,1536]{2,1,0:T(2,128)S(1)}, u32[]{:S(2)}, u32[]{:S(2)}) collective-permute-start(f32[1,2,1536]{2,1,0:T(2,128)S(1)} %maximum_bitcast_fusion.1), channel_id=1, source_target_pairs={{2,0},{4,2},{6,4},{8,6},{10,8},{12,10},{14,12},{3,1},{5,3},{7,5},{... | collective-permute-start | bytes 36872 | tf_op jit(solution)/shard_map/ppermute | solution.py:28
  165.1 5.2 %collective-permute-start.8 = (f32[1,1,1536]{2,1,0:T(1,128)S(1)}, f32[1,1,1536]{2,1,0:T(1,128)S(1)}, u32[]{:S(2)}, u32[]{:S(2)}) collective-permute-start(f32[1,1,1536]{2,1,0:T(1,128)S(1)} %get-tuple-element.133), channel_id=1, source_target_pairs={{0,2},{2,4},{4,6},{6,8},{8,10},{10,12},{12,14},{1,3},{3,5},{5,7},{... | collective-permute-start | bytes 18440 | tf_op jit(solution)/shard_map/ppermute | solution.py:25
  169.0 5.5 %collective-permute-start.9 = (f32[1,1,1536]{2,1,0:T(1,128)S(1)}, f32[1,1,1536]{2,1,0:T(1,128)S(1)}, u32[]{:S(2)}, u32[]{:S(2)}) collective-permute-start(f32[1,1,1536]{2,1,0:T(1,128)S(1)} %get-tuple-element.133), channel_id=1, source_target_pairs={{2,0},{4,2},{6,4},{8,6},{10,8},{12,10},{14,12},{3,1},{5,3},{7,5},{... | collective-permute-start | bytes 18440 | tf_op jit(solution)/shard_map/ppermute | solution.py:28
  174.5 4.6 %collective-permute-start.11 = (f32[3,1,1536]{2,1,0:T(1,128)S(1)}, f32[3,1,1536]{2,1,0:T(1,128)S(1)}, u32[]{:S(2)}, u32[]{:S(2)}) collective-permute-start(f32[3,1,1536]{2,1,0:T(1,128)S(1)} %pad_maximum_fusion.5), channel_id=1, source_target_pairs={{1,0},{3,2},{5,4},{7,6},{9,8},{11,10},{13,12},{15,14},{17,16},{19,... | collective-permute-start | bytes 55304 | tf_op jit(solution)/shard_map/ppermute | solution.py:28
  175.8 3.9 collective-permute-start.10
  192.7 5.6 %collective-permute-start.12 = (f32[1,2,1536]{2,1,0:T(2,128)S(1)}, f32[1,2,1536]{2,1,0:T(2,128)S(1)}, u32[]{:S(2)}, u32[]{:S(2)}) collective-permute-start(f32[1,2,1536]{2,1,0:T(2,128)S(1)} %maximum_bitcast_fusion.2), channel_id=1, source_target_pairs={{0,2},{2,4},{4,6},{6,8},{8,10},{10,12},{12,14},{1,3},{3,5},{5,7},{... | collective-permute-start | bytes 36872 | tf_op jit(solution)/shard_map/ppermute | solution.py:25
  197.0 5.6 %collective-permute-start.13 = (f32[1,2,1536]{2,1,0:T(2,128)S(1)}, f32[1,2,1536]{2,1,0:T(2,128)S(1)}, u32[]{:S(2)}, u32[]{:S(2)}) collective-permute-start(f32[1,2,1536]{2,1,0:T(2,128)S(1)} %maximum_bitcast_fusion.3), channel_id=1, source_target_pairs={{2,0},{4,2},{6,4},{8,6},{10,8},{12,10},{14,12},{3,1},{5,3},{7,5},{... | collective-permute-start | bytes 36872 | tf_op jit(solution)/shard_map/ppermute | solution.py:28
  202.7 4.4 %collective-permute-start.15 = (f32[4,1,1536]{2,1,0:T(1,128)S(1)}, f32[4,1,1536]{2,1,0:T(1,128)S(1)}, u32[]{:S(2)}, u32[]{:S(2)}) collective-permute-start(f32[4,1,1536]{2,1,0:T(1,128)S(1)} %get-tuple-element.107), channel_id=1, source_target_pairs={{1,0},{3,2},{5,4},{7,6},{9,8},{11,10},{13,12},{15,14},{17,16},{19,... | collective-permute-start | bytes 73736 | tf_op jit(solution)/shard_map/ppermute | solution.py:28
  204.0 3.9 collective-permute-start.14
  241.6 5.5 %collective-permute-start.17 = (f32[1,1,1536]{2,1,0:T(1,128)S(1)}, f32[1,1,1536]{2,1,0:T(1,128)S(1)}, u32[]{:S(2)}, u32[]{:S(2)}) collective-permute-start(f32[1,1,1536]{2,1,0:T(1,128)S(1)} %get-tuple-element.94), channel_id=1, source_target_pairs={{2,0},{4,2},{6,4},{8,6},{10,8},{12,10},{14,12},{3,1},{5,3},{7,5},{... | collective-permute-start | bytes 18440 | tf_op jit(solution)/shard_map/ppermute | solution.py:28
  247.1 4.4 %collective-permute-start.19 = (f32[3,1,1536]{2,1,0:T(1,128)S(1)}, f32[3,1,1536]{2,1,0:T(1,128)S(1)}, u32[]{:S(2)}, u32[]{:S(2)}) collective-permute-start(f32[3,1,1536]{2,1,0:T(1,128)S(1)} %pad_maximum_fusion.6), channel_id=1, source_target_pairs={{1,0},{3,2},{5,4},{7,6},{9,8},{11,10},{13,12},{15,14},{17,16},{19,... | collective-permute-start | bytes 55304 | tf_op jit(solution)/shard_map/ppermute | solution.py:28
  267.1 5.6 %collective-permute-start.21 = (f32[1,2,1536]{2,1,0:T(2,128)S(1)}, f32[1,2,1536]{2,1,0:T(2,128)S(1)}, u32[]{:S(2)}, u32[]{:S(2)}) collective-permute-start(f32[1,2,1536]{2,1,0:T(2,128)S(1)} %maximum_bitcast_fusion.5), channel_id=1, source_target_pairs={{2,0},{4,2},{6,4},{8,6},{10,8},{12,10},{14,12},{3,1},{5,3},{7,5},{... | collective-permute-start | bytes 36872 | tf_op jit(solution)/shard_map/ppermute | solution.py:28
  272.7 4.4 %collective-permute-start.23 = (f32[4,1,1536]{2,1,0:T(1,128)S(1)}, f32[4,1,1536]{2,1,0:T(1,128)S(1)}, u32[]{:S(2)}, u32[]{:S(2)}) collective-permute-start(f32[4,1,1536]{2,1,0:T(1,128)S(1)} %get-tuple-element.105), channel_id=1, source_target_pairs={{1,0},{3,2},{5,4},{7,6},{9,8},{11,10},{13,12},{15,14},{17,16},{19,... | collective-permute-start | bytes 73736 | tf_op jit(solution)/shard_map/ppermute | solution.py:28
  274.0 3.9 collective-permute-start.22
  315.2 5.5 %collective-permute-start.25 = (f32[1,1,1536]{2,1,0:T(1,128)S(1)}, f32[1,1,1536]{2,1,0:T(1,128)S(1)}, u32[]{:S(2)}, u32[]{:S(2)}) collective-permute-start(f32[1,1,1536]{2,1,0:T(1,128)S(1)} %multiply_subtract_fusion.2), channel_id=1, source_target_pairs={{2,0},{4,2},{6,4},{8,6},{10,8},{12,10},{14,12},{3,1},{5,3},{7,5},{... | collective-permute-start | bytes 18440 | tf_op jit(solution)/shard_map/ppermute | solution.py:28
  320.7 4.6 %collective-permute-start.27 = (f32[3,1,1536]{2,1,0:T(1,128)S(1)}, f32[3,1,1536]{2,1,0:T(1,128)S(1)}, u32[]{:S(2)}, u32[]{:S(2)}) collective-permute-start(f32[3,1,1536]{2,1,0:T(1,128)S(1)} %pad_maximum_fusion.7), channel_id=1, source_target_pairs={{1,0},{3,2},{5,4},{7,6},{9,8},{11,10},{13,12},{15,14},{17,16},{19,... | collective-permute-start | bytes 55304 | tf_op jit(solution)/shard_map/ppermute | solution.py:28
  322.0 3.9 collective-permute-start.26
  340.6 5.6 %collective-permute-start.29 = (f32[1,2,1536]{2,1,0:T(2,128)S(1)}, f32[1,2,1536]{2,1,0:T(2,128)S(1)}, u32[]{:S(2)}, u32[]{:S(2)}) collective-permute-start(f32[1,2,1536]{2,1,0:T(2,128)S(1)} %maximum_bitcast_fusion.7), channel_id=1, source_target_pairs={{2,0},{4,2},{6,4},{8,6},{10,8},{12,10},{14,12},{3,1},{5,3},{7,5},{... | collective-permute-start | bytes 36872 | tf_op jit(solution)/shard_map/ppermute | solution.py:28
  346.3 4.4 %collective-permute-start.31 = (f32[4,1,1536]{2,1,0:T(1,128)S(1)}, f32[4,1,1536]{2,1,0:T(1,128)S(1)}, u32[]{:S(2)}, u32[]{:S(2)}) collective-permute-start(f32[4,1,1536]{2,1,0:T(1,128)S(1)} %get-tuple-element.103), channel_id=1, source_target_pairs={{1,0},{3,2},{5,4},{7,6},{9,8},{11,10},{13,12},{15,14},{17,16},{19,... | collective-permute-start | bytes 73736 | tf_op jit(solution)/shard_map/ppermute | solution.py:28
  347.6 3.9 collective-permute-start.30
  (16 other events, 257.1 us)
where the time goes:
time: 388 us; the launch traced here: 387 us
  matrix products  146 us (38%)
  blocking collectives  91.4 us (24%)
  starting transfers between devices  65.4 us (17%)
  waiting for transfers between devices  44.1 us (11%)
  local copies, waits for them, and re-layouts  19.7 us (5%)
  between operations  11.6 us (3%)
  other arithmetic  8.56 us (2%)
    psum x3, blocking collectives, two_products(): lax.psum((jnp.sum(residual * residual), jnp.sum(residual * image)), ('tx'...  91.4 us
    dot_general x6, matrix products, evaluate(): jnp.einsum('pkc,k->pc', amplitude * amplitude, weight_pair, precision=lax...  73.3 us
    ppermute x16, starting transfers between devices, extended_2(): lax.ppermute(lax.slice_in_dim(block, block.shape[dim] - width, None, axis...  44.7 us
    ppermute x16, waiting for transfers between devices, extended_2(): lax.ppermute(lax.slice_in_dim(block, 0, width, axis=dim), axis, backward)  30.8 us
    dot_general x6, matrix products, evaluate(): jnp.dot(row_piece, kernels, preferred_element_type=jnp.float32)  26.9 us
    dot_general x3, matrix products, forward(): jnp.einsum('nkij,nkj->ni', jac_blocks, gathered, precision=lax.Precision....  21.8 us
    ppermute x16, starting transfers between devices, extended_2(): lax.ppermute(lax.slice_in_dim(block, 0, width, axis=dim), axis, backward)  20.7 us
    dot_general x4, matrix products, backward(): jnp.einsum('nkij,ni->nkj', jac_blocks, values.reshape(pt_blocks, BS), pre...  20.3 us
  transfers between devices with their start and end apart: 32, of which 15 were waited for; matrix products, arithmetic and copies ran while one was open for 2% of the time, Pallas kernels for 0%

commit v1 on v0

v1 whole, which is shorter than its diff:
```python
import functools

import jax
import jax.numpy as jnp
from jax import lax
from jax.experimental import pallas as pl
from jax.experimental.pallas import tpu as pltpu
from jax.sharding import PartitionSpec as P

BS = 128
SEG = 1536
ROWS = 16
MESH = pl.DeviceIdType.MESH
SIDES = ((0, 0), (-1, 0), (1, 0), (0, -1), (0, 1))
OPPOSITE = (0, 2, 1, 4, 3)
ITERS = 3


def split_3(value):
    high = value.astype(jnp.bfloat16)
    rest = value - high.astype(jnp.float32)
    middle = rest.astype(jnp.bfloat16)
    low = (rest - middle.astype(jnp.float32)).astype(jnp.bfloat16)
    return high, middle, low


def split_2(value):
    high = value.astype(jnp.bfloat16)
    low = (value - high.astype(jnp.float32)).astype(jnp.bfloat16)
    return high, low


def select_3(chooser, value):
    parts = split_3(value)
    total = jnp.dot(chooser, parts[2], preferred_element_type=jnp.float32)
    total = total + jnp.dot(chooser, parts[1], preferred_element_type=jnp.float32)
    return total + jnp.dot(chooser, parts[0], preferred_element_type=jnp.float32)


def kernel(
    n_tx,
    n_ty,
    raster_hbm,
    kernels_hbm,
    kw_ref,
    cw_ref,
    need_ref,
    slot_ref,
    row_ref,
    level_ref,
    weight_ref,
    ids_ref,
    jac_hbm,
    epe_ref,
    step_ref,
    raster_v,
    kernels_v,
    jac_v,
    q_own,
    edge_x,
    edge_y,
    halo_x,
    halo_y,
    q_ext,
    need_pad,
    choose,
    vec,
    gathered,
    contrib,
    w_cols,
    u_cols,
    w_pad,
    sent,
    arrived,
    part_sums,
    all_sums,
    local_sem,
    hx_send,
    hx_recv,
    hy_send,
    hy_recv,
    ex_send,
    ex_recv,
    sum_send,
    sum_recv,
):
    n_dev = n_tx * n_ty
    gx, gy = raster_hbm.shape[0], raster_hbm.shape[1]
    pt_blocks = slot_ref.shape[1] // BS
    nnz = ids_ref.shape[1]
    seg_blocks = step_ref.shape[1] // BS
    n_kern = kw_ref.shape[0]
    span_y = gy + 2
    need = need_ref.shape[1]
    tx, ty = lax.axis_index("tx"), lax.axis_index("ty")
    rank = tx * n_ty + ty

    copy_k = pltpu.make_async_copy(kernels_hbm, kernels_v, local_sem.at[0])
    copy_r = pltpu.make_async_copy(raster_hbm, raster_v, local_sem.at[1])
    copy_j = pltpu.make_async_copy(jac_hbm, jac_v, local_sem.at[2])
    copy_k.start()
    copy_r.start()
    copy_j.start()

    def present(dx, dy):
        ok = None
        for pos, delta, count in ((tx, dx, n_tx), (ty, dy, n_ty)):
            test = None
            if delta < 0:
                test = pos + delta >= 0
            elif delta > 0:
                test = pos + delta < count
            if test is not None:
                ok = test if ok is None else jnp.logical_and(ok, test)
        return ok

    halo_x[...] = jnp.zeros_like(halo_x)
    halo_y[...] = jnp.zeros_like(halo_y)
    arrived[...] = jnp.zeros_like(arrived)

    barrier = pltpu.get_barrier_semaphore()

    def other(offset):
        peer = lax.rem(rank + offset, n_dev)
        return peer, {"tx": peer // n_ty, "ty": lax.rem(peer, n_ty)}

    @pl.loop(1, n_dev)
    def _(offset):
        pl.semaphore_signal(barrier, inc=1, device_id=other(offset)[1], device_id_type=MESH)

    copy_k.wait()
    cut = cw_ref[...]
    both = jnp.zeros((2 * BS, BS), jnp.float32)
    width = 4 * BS
    for chunk in range(2 * n_kern * BS // width):
        piece = kernels_v[:, chunk * width : (chunk + 1) * width]
        factor = jnp.concatenate(
            [cut * kw_ref[(chunk * 4 + i) // 2] for i in range(4)], axis=1
        )
        high, low = split_2(piece.astype(jnp.float32) * factor)
        both = both + lax.dot_general(
            jnp.concatenate([high, low], axis=0),
            piece,
            (((1,), (1,)), ((), ())),
            preferred_element_type=jnp.float32,
        )
    form = jnp.concatenate(split_2(both[:BS] + both[BS:]), axis=1)

    copy_r.wait()
    eye = lax.broadcasted_iota(jnp.int32, (1, BS, BS), 1) == lax.broadcasted_iota(
        jnp.int32, (1, BS, BS), 2
    )

    @pl.loop(0, gx)
    def _(a):
        rows = raster_v[a].reshape(gy * BS, BS)
        product = jnp.dot(rows, form, preferred_element_type=jnp.float32)
        terms = (product[:, :BS] + product[:, BS:]) * rows.astype(jnp.float32)
        column = jnp.sum(terms.reshape(gy, BS, BS), axis=2, keepdims=True)
        q = jnp.sum(jnp.where(eye, column, 0.0), axis=1)
        q_own[a] = q
        edge_y[0, pl.ds(a, 1), :] = q[0:1]
        edge_y[1, pl.ds(a, 1), :] = q[gy - 1 : gy]

    edge_x[0] = q_own[0]
    edge_x[1] = q_own[gx - 1]

    pl.semaphore_wait(barrier, n_dev - 1)

    halo_copies = []
    for side, dx in ((0, -1), (1, 1)):
        for dy in (-1, 0, 1):
            halo_copies.append(
                (
                    (dx, dy),
                    pltpu.make_async_remote_copy(
                        src_ref=edge_x.at[side],
                        dst_ref=halo_x.at[1 - side, 1 - dy],
                        send_sem=hx_send.at[side, 1 + dy],
                        recv_sem=hx_recv.at[1 - side, 1 - dy],
                        device_id={"tx": tx + dx, "ty": ty + dy},
                        device_id_type=MESH,
                    ),
                )
            )
    for side, dy in ((0, -1), (1, 1)):
        halo_copies.append(
            (
                (0, dy),
                pltpu.make_async_remote_copy(
                    src_ref=edge_y.at[side],
                    dst_ref=halo_y.at[1 - side],
                    send_sem=hy_send.at[side],
                    recv_sem=hy_recv.at[1 - side],
                    device_id={"tx": tx, "ty": ty + dy},
                    device_id_type=MESH,
                ),
            )
        )
    for (dx, dy), copy in halo_copies:

        @pl.when(present(dx, dy))
        def _():
            copy.start()

    q_ext[...] = jnp.zeros_like(q_ext)
    for a in range(gx):
        start = (a + 1) * span_y + 1
        q_ext[start : start + gy, :] = q_own[a]
    need_pad[...] = jnp.full(need_pad.shape, -1, jnp.int32)
    need_pad[:, :need] = need_ref[...]
    listed = (lax.broadcasted_iota(jnp.int32, (BS, BS), 0) == need_pad[...]).astype(jnp.float32).astype(
        jnp.bfloat16
    )
    choose[...] = jnp.zeros_like(choose)
    ids = ids_ref[...]
    for t in range(1, 5):
        ids = ids + jnp.where(ids_ref[...] >= t * seg_blocks, ROWS - seg_blocks, 0)
    for k in range(nnz):
        choose[k * pt_blocks : (k + 1) * pt_blocks, :] = (
            lax.broadcasted_iota(jnp.int32, (pt_blocks, BS), 1) == ids[:, k : k + 1]
        ).astype(jnp.float32)
    pick = choose[...].astype(jnp.bfloat16)
    pick_t = choose[...].T.astype(jnp.bfloat16)
    contrib[...] = jnp.zeros_like(contrib)
    vec[...] = jnp.zeros_like(vec)
    w_pad[...] = jnp.zeros_like(w_pad)
    for n in range(pt_blocks):
        w_pad[n : n + 1, :] = weight_ref[:, n * BS : (n + 1) * BS]
    turned = w_pad[...].T
    for n in range(pt_blocks):
        w_cols[n] = jnp.broadcast_to(turned[:, n : n + 1], (BS, BS))

    for side, dx in ((0, -1), (1, 1)):
        for dy in (-1, 0, 1):

            @pl.when(present(dx, dy))
            def _():
                pltpu.make_async_remote_copy(
                    src_ref=edge_x.at[side],
                    dst_ref=halo_x.at[side, 1 + dy],
                    send_sem=hx_send.at[side, 1 + dy],
                    recv_sem=hx_recv.at[side, 1 + dy],
                    device_id={"tx": tx + dx, "ty": ty + dy},
                    device_id_type=MESH,
                ).wait_recv()

    for side, dy in ((0, -1), (1, 1)):

        @pl.when(present(0, dy))
        def _():
            pltpu.make_async_remote_copy(
                src_ref=edge_y.at[side],
                dst_ref=halo_y.at[side],
                send_sem=hy_send.at[side],
                recv_sem=hy_recv.at[side],
                device_id={"tx": tx, "ty": ty + dy},
                device_id_type=MESH,
            ).wait_recv()

    for side in (0, 1):
        base = 0 if side == 0 else (gx + 1) * span_y
        q_ext[base + 1 : base + 1 + gy, :] = halo_x[side, 1]
        q_ext[base : base + 1, :] = halo_x[side, 0, gy - 1 : gy, :]
        q_ext[base + gy + 1 : base + gy + 2, :] = halo_x[side, 2, 0:1, :]
        for a in range(gx):
            at = (a + 1) * span_y + (0 if side == 0 else gy + 1)
            q_ext[at : at + 1, :] = halo_y[side, a : a + 1, :]

    table = jnp.concatenate(split_2(q_ext[...].T), axis=0)
    table = jnp.dot(table, listed, preferred_element_type=jnp.float32).astype(jnp.bfloat16)
    group = 2 * BS
    position = lax.broadcasted_iota(jnp.int32, (BS, group), 0)
    for piece in range(pt_blocks * BS // group):
        part = slice(piece * group, (piece + 1) * group)
        entry = (position == slot_ref[:, part]).astype(jnp.float32).astype(jnp.bfloat16)
        found = jnp.dot(table, entry, preferred_element_type=jnp.float32)
        found = found[:BS] + found[BS:]
        value = jnp.sum(
            jnp.where(position == row_ref[:, part], found, 0.0), axis=0, keepdims=True
        )
        error = value - level_ref[:, part]
        epe_ref[:, part] = error
        pulled = error * weight_ref[:, part]
        for i in range(group // BS):
            n = piece * (group // BS) + i
            w_pad[n : n + 1, :] = pulled[:, i * BS : (i + 1) * BS]
    turned = w_pad[...].T
    for n in range(pt_blocks):
        u_cols[n] = jnp.broadcast_to(turned[:, n : n + 1], (BS, BS))

    copy_j.wait()

    def part_copy(turn, t, t_here):
        return pltpu.make_async_remote_copy(
            src_ref=sent.at[turn, t],
            dst_ref=arrived.at[turn, t_here],
            send_sem=ex_send.at[turn, t],
            recv_sem=ex_recv.at[turn, t_here],
            device_id={"tx": tx + SIDES[t][0], "ty": ty + SIDES[t][1]},
            device_id_type=MESH,
        )

    def exchange(turn, parts):
        for t in range(1, 5):
            sent[turn, t] = parts[t]
        for t in range(1, 5):

            @pl.when(present(*SIDES[t]))
            def _():
                part_copy(turn, t, OPPOSITE[t]).start()

    def receive(turn):
        for t in range(1, 5):

            @pl.when(present(*SIDES[t]))
            def _():
                part_copy(turn, t, t).wait_recv()

        return [arrived[turn, t] for t in range(1, 5)]

    def finish(turn):
        summed = select_3(pick_t, contrib[...])
        parts = [summed[t * ROWS : (t + 1) * ROWS] for t in range(5)]
        exchange(turn, parts)
        others = receive(turn)
        return parts[0] + (others[0] + others[1]) + (others[2] + others[3])

    @pl.loop(0, pt_blocks)
    def _(n):
        for k in range(nnz):
            contrib[pl.ds(k * pt_blocks + n, 1), :] = jnp.sum(
                jac_v[n, k] * u_cols[n], axis=0, keepdims=True
            )

    def spread(own, others):
        vec[0:ROWS, :] = own
        for t in range(1, 5):
            vec[t * ROWS : (t + 1) * ROWS, :] = others[t - 1]

    def apply_normal(turn, own):
        gathered[...] = select_3(pick, vec[...])

        @pl.loop(0, pt_blocks)
        def _(n):
            total = jac_v[n, 0] * gathered[pl.ds(n, 1), :]
            for k in range(1, nnz):
                total = total + jac_v[n, k] * gathered[pl.ds(k * pt_blocks + n, 1), :]
            scaled = jnp.sum(total, axis=1, keepdims=True) * w_cols[n]
            for k in range(nnz):
                contrib[pl.ds(k * pt_blocks + n, 1), :] = jnp.sum(
                    jac_v[n, k] * scaled, axis=0, keepdims=True
                )

        return finish(turn) + own

    def sum_copy(turn, offset):
        peer, where = other(offset)
        return pltpu.make_async_remote_copy(
            src_ref=part_sums.at[turn],
            dst_ref=all_sums.at[turn, rank],
            send_sem=sum_send.at[turn, offset],
            recv_sem=sum_recv.at[turn, rank],
            device_id=where,
            device_id_type=MESH,
        )

    def start_sums(turn, residual, image):
        both = jnp.concatenate(
            [
                jnp.sum(residual * residual, axis=0, keepdims=True),
                jnp.sum(residual * image, axis=0, keepdims=True),
            ],
            axis=0,
        )
        part_sums[turn] = both
        all_sums[turn, rank] = both

        @pl.loop(1, n_dev)
        def _(offset):
            sum_copy(turn, offset).start()

    def end_sums(turn):
        @pl.loop(1, n_dev)
        def _(offset):
            peer, where = other(offset)
            pltpu.make_async_remote_copy(
                src_ref=part_sums.at[turn],
                dst_ref=all_sums.at[turn, peer],
                send_sem=sum_send.at[turn, offset],
                recv_sem=sum_recv.at[turn, peer],
                device_id=where,
                device_id_type=MESH,
            ).wait_recv()

        total = jnp.sum(jnp.sum(all_sums[turn], axis=0), axis=1, keepdims=True)
        return total[0:1], total[1:2]

    residual = -finish(0)
    exchange(1, [residual] * 5)
    spread(residual, receive(1))
    image = apply_normal(2, residual)
    start_sums(0, residual, image)
    exchange(3, [image] * 5)
    image_others = receive(3)
    spread(image, image_others)
    second = apply_normal(4, image)
    exchange(5, [second] * 5)

    norm_now, product = end_sums(0)
    alpha = norm_now / product
    direction, along, beyond = residual, image, second
    step = alpha * direction
    residual = residual - alpha * along
    image = image - alpha * beyond
    start_sums(1, residual, image)
    second_others = receive(5)
    spread(image, [w - alpha * z for w, z in zip(image_others, second_others)])
    second = apply_normal(6, image)

    norm_next, product = end_sums(1)
    ratio = norm_next / norm_now
    alpha = norm_next / (product - ratio * norm_next / alpha)
    norm_now = norm_next
    direction = residual + ratio * direction
    along = image + ratio * along
    beyond = second + ratio * beyond
    step = step + alpha * direction
    residual = residual - alpha * along
    image = image - alpha * beyond
    start_sums(2, residual, image)

    for (dx, dy), copy in halo_copies:

        @pl.when(present(dx, dy))
        def _():
            copy.wait_send()

    for turn in range(7):
        for t in range(1, 5):

            @pl.when(present(*SIDES[t]))
            def _():
                part_copy(turn, t, OPPOSITE[t]).wait_send()

    for turn in range(3):

        @pl.loop(1, n_dev)
        def _(offset):
            sum_copy(turn, offset).wait_send()

    norm_next, product = end_sums(2)
    ratio = norm_next / norm_now
    alpha = norm_next / (product - ratio * norm_next / alpha)
    direction = residual + ratio * direction
    step = step + alpha * direction
    for j in range(seg_blocks):
        step_ref[:, j * BS : (j + 1) * BS] = step[j : j + 1, :]


def on_device(
    n_tx,
    n_ty,
    raster,
    kernels,
    kernel_weights,
    cut_weights,
    need_list,
    point_slot,
    point_row,
    threshold,
    point_weight,
    jac_ids,
    jacobian,
):
    points = point_slot.shape[-1]
    pt_blocks, nnz = jac_ids.shape[-2:]
    gx, gy = raster.shape[:2]
    segments = SEG
    n_dev = n_tx * n_ty
    f32 = jnp.float32
    vmem = pl.BlockSpec(memory_space=pltpu.VMEM)
    anywhere = pl.BlockSpec(memory_space=pl.ANY)
    smem = pl.BlockSpec(memory_space=pltpu.SMEM)
    dma = pltpu.SemaphoreType.DMA
    epe, step = pl.pallas_call(
        functools.partial(kernel, n_tx, n_ty),
        out_shape=(
            jax.ShapeDtypeStruct((1, points), f32),
            jax.ShapeDtypeStruct((1, segments), f32),
        ),
        in_specs=[anywhere, anywhere, smem] + [vmem] * 7 + [anywhere],
        out_specs=(vmem, vmem),
        scratch_shapes=[
            pltpu.VMEM(raster.shape, jnp.bfloat16),
            pltpu.VMEM(kernels.shape, jnp.bfloat16),
            pltpu.VMEM((pt_blocks, nnz, BS, BS), f32),
            pltpu.VMEM((gx, gy, BS), f32),
            pltpu.VMEM((2, gy, BS), f32),
            pltpu.VMEM((2, gx, BS), f32),
            pltpu.VMEM((2, 3, gy, BS), f32),
            pltpu.VMEM((2, gx, BS), f32),
            pltpu.VMEM((BS, BS), f32),
            pltpu.VMEM((1, BS), jnp.int32),
            pltpu.VMEM((BS, BS), f32),
            pltpu.VMEM((BS, BS), f32),
            pltpu.VMEM((BS, BS), f32),
            pltpu.VMEM((BS, BS), f32),
            pltpu.VMEM((pt_blocks, BS, BS), f32),
            pltpu.VMEM((pt_blocks, BS, BS), f32),
            pltpu.VMEM((BS, BS), f32),
            pltpu.VMEM((7, 5, ROWS, BS), f32),
            pltpu.VMEM((7, 5, ROWS, BS), f32),
            pltpu.VMEM((3, 2, BS), f32),
            pltpu.VMEM((3, n_dev, 2, BS), f32),
            dma((3,)),
            dma((2, 3)),
            dma((2, 3)),
            dma((2,)),
            dma((2,)),
            dma((7, 5)),
            dma((7, 5)),
            dma((3, n_dev)),
            dma((3, n_dev)),
        ],
        compiler_params=pltpu.CompilerParams(
            collective_id=0, has_side_effects=True, vmem_limit_bytes=48 * 1024 * 1024
        ),
    )(
        raster,
        kernels,
        kernel_weights,
        cut_weights.reshape(1, BS),
        need_list.reshape(1, -1),
        point_slot.reshape(1, points),
        point_row.reshape(1, points),
        threshold.reshape(1, points),
        point_weight.reshape(1, points),
        jac_ids.reshape(pt_blocks, nnz),
        jacobian.reshape(pt_blocks, nnz, BS, BS),
    )
    return epe.reshape(1, 1, points), step.reshape(1, 1, segments)


def solution(mesh):
    tiles = ("grp", "tx")
    in_specs = (
        P(tiles, "ty", None, None),
        P(),
        P(),
        P(),
        P(tiles, "ty", None),
        P(tiles, "ty", None),
        P(tiles, "ty", None),
        P(tiles, "ty", None),
        P(tiles, "ty", None),
        P(tiles, "ty", None, None),
        P(tiles, "ty", None, None, None, None),
    )
    out_specs = (P(tiles, "ty", None), P(tiles, "ty", None))
    return jax.shard_map(
        functools.partial(on_device, mesh.shape["tx"], mesh.shape["ty"]),
        mesh=mesh,
        in_specs=in_specs,
        out_specs=out_specs,
        check_vma=False,
    )
```

time: 388 us -> 61.5 us (0.16)
  matrix products: 146 us -> 0 us
  blocking collectives: 91.4 us -> 0 us
  starting transfers between devices: 65.4 us -> 0 us
  Pallas kernels: 0 us -> 50.8 us
  waiting for transfers between devices: 44.1 us -> 0 us
  between operations: 11.6 us -> 0.65 us
  local copies, waits for them, and re-layouts: 19.7 us -> 9.56 us
  other arithmetic: 8.56 us -> 0 us
    dot_general x32 -> x0, matrix products: 146 us -> none  [the longest x6 73.3 us: evaluate(): jnp.einsum('pkc,k->pc', amplitude * amplitude, weight_pair, precision=lax...]
    psum x3 -> x0, blocking collectives: 91.4 us -> none  [two_products(): lax.psum((jnp.sum(residual * residual), jnp.sum(residual * image)), ('tx'...]
    ppermute x32 -> x0, starting transfers between devices: 65.4 us -> none  [the longest x16 44.7 us: extended_2(): lax.ppermute(lax.slice_in_dim(block, block.shape[dim] - width, None, axis...]
    pallas_call x0 -> x1, Pallas kernels: none -> 50.8 us  [on_device(): pl.pallas_call(functools.partial(kernel, n_tx, n_ty), out_shape=(jax.Shap...]
    ppermute x32 -> x0, waiting for transfers between devices: 44.1 us -> none  [the longest x16 30.8 us: extended_2(): lax.ppermute(lax.slice_in_dim(block, 0, width, axis=dim), axis, backward)]
    gather x1 -> x0, local copies, waits for them, and re-layouts: 10.7 us -> none  [on_device(): row_data = extended.reshape(-1, BS)[blocks * BS + rows_in]]
    concatenate x8 -> x0, other arithmetic: 3.97 us -> none  [extended_2(): block = jnp.concatenate([low, block, high], axis=dim)]
    unnamed x37 -> x20, local copies, waits for them, and re-layouts: 4.93 us -> 8.8 us
  transfers between devices with their start and end apart: 32 -> 0, of which waited for: 15 -> 0; matrix products, arithmetic and copies ran while one was open for 2% -> 0% of each run, Pallas kernels for 0% -> 0%
where the time goes in v1:
time: 61.5 us; the launch traced here: 61 us
  Pallas kernels  50.8 us (83%)
  local copies, waits for them, and re-layouts  9.56 us (16%)
  between operations  0.65 us (1%)
    pallas_call x1, Pallas kernels, on_device(): pl.pallas_call(functools.partial(kernel, n_tx, n_ty), out_shape=(jax.Shap...  50.8 us
    unnamed x20, local copies, waits for them, and re-layouts  8.8 us

profile of v1, /device:TPU:0, one launch (start us, length us, event | category | flops | bytes accessed | tf_op | source)
XLA Modules:
  0.0 61.0 jit_solution(2726570569800553260)
XLA Ops:
  0.6 0.8 %copy.13.ids_ref = s32[24,4]{1,0:T(8,128)S(1)} copy(s32[24,4]{0,1:T(4,128)} %bitcast.19) | data formatting | bytes 768 | tf_op jit(solution)/shard_map/reshape | solution.py:539
  1.4 0.0 copy-start
  1.4 1.6 %copy-done = bf16[8,8,128,128]{3,2,1,0:T(8,128)(2,1)S(1)} copy-done((bf16[8,8,128,128]{3,2,1,0:T(8,128)(2,1)S(1)}, bf16[8,8,128,128]{3,2,1,0:T(8,128)(2,1)}, u32[]{:S(2)}) %copy-start) | copy-done | bytes 2097176
  3.0 0.0 copy-start.1
  3.0 1.2 %copy-done.1 = bf16[128,4096]{1,0:T(8,128)(2,1)S(1)} copy-done((bf16[128,4096]{1,0:T(8,128)(2,1)S(1)}, bf16[128,4096]{1,0:T(8,128)(2,1)}, u32[]{:S(2)}) %copy-start.1) | copy-done | bytes 1048600
  4.2 0.0 copy-start.2
  4.2 0.7 %copy-done.2 = s32[1,1,3072]{2,1,0:T(1,128)S(1)} copy-done((s32[1,1,3072]{2,1,0:T(1,128)S(1)}, s32[1,1,3072]{2,1,0:T(1,128)}, u32[]{:S(2)}) %copy-start.2) | copy-done | bytes 12312
  4.9 0.0 copy-start.3
  4.9 0.7 %copy-done.3 = s32[1,1,3072]{2,1,0:T(1,128)S(1)} copy-done((s32[1,1,3072]{2,1,0:T(1,128)S(1)}, s32[1,1,3072]{2,1,0:T(1,128)}, u32[]{:S(2)}) %copy-start.3) | copy-done | bytes 12312
  5.6 0.0 copy-start.4
  5.6 0.7 %copy-done.4 = f32[1,1,3072]{2,1,0:T(1,128)S(1)} copy-done((f32[1,1,3072]{2,1,0:T(1,128)S(1)}, f32[1,1,3072]{2,1,0:T(1,128)}, u32[]{:S(2)}) %copy-start.4) | copy-done | bytes 12312
  6.3 0.0 copy-start.5
  6.3 0.7 %copy-done.5 = f32[1,1,3072]{2,1,0:T(1,128)S(1)} copy-done((f32[1,1,3072]{2,1,0:T(1,128)S(1)}, f32[1,1,3072]{2,1,0:T(1,128)}, u32[]{:S(2)}) %copy-start.5) | copy-done | bytes 12312
  7.0 0.0 copy-start.6
  7.0 0.7 %copy-done.6 = f32[16]{0:T(128)S(1)} copy-done((f32[16]{0:T(128)S(1)}, f32[16]{0:T(128)}, u32[]{:S(2)}) %copy-start.6) | copy-done | bytes 88
  7.7 0.0 copy-start.7
  7.7 0.7 %copy-done.7 = f32[128]{0:T(128)S(1)} copy-done((f32[128]{0:T(128)S(1)}, f32[128]{0:T(128)}, u32[]{:S(2)}) %copy-start.7) | copy-done | bytes 536
  8.3 0.0 copy-start.8
  8.4 0.7 %copy-done.8 = s32[1,1,84]{2,1,0:T(1,128)S(1)} copy-done((s32[1,1,84]{2,1,0:T(1,128)S(1)}, s32[1,1,84]{2,1,0:T(1,128)}, u32[]{:S(2)}) %copy-start.8) | copy-done | bytes 360
  9.0 50.8 %shard_map.122 = (f32[1,3072]{1,0:T(1,128)S(1)}, f32[1,1536]{1,0:T(1,128)S(1)}) custom-call(bf16[8,8,128,128]{3,2,1,0:T(8,128)(2,1)S(1)} %copy-done, bf16[128,4096]{1,0:T(8,128)(2,1)S(1)} %copy-done.1, f32[16]{0:T(128)S(1)} %copy-done.6, f32[1,128]{1,0:T(1,128)S(1)} %bitcast.16, s32[1,84]{1,0:T(1,128)S(1)} %bitcast.17, s32[1,3072]{1,0:T(1,128)S(1)} %bitcast.11, ...), custom_call_target="tpu_custom_call" | custom-call | tf_op jit(solution)/shard_map/pallas_call | solution.py:486
  59.9 0.6 copy.16
  60.5 0.6 copy.17
Async XLA Ops:
  1.4 1.6 %copy-start = (bf16[8,8,128,128]{3,2,1,0:T(8,128)(2,1)S(1)}, bf16[8,8,128,128]{3,2,1,0:T(8,128)(2,1)}, u32[]{:S(2)}) copy-start(bf16[8,8,128,128]{3,2,1,0:T(8,128)(2,1)} %raster_hbm.1) | copy-start | bytes 6291460
  3.0 1.2 %copy-start.1 = (bf16[128,4096]{1,0:T(8,128)(2,1)S(1)}, bf16[128,4096]{1,0:T(8,128)(2,1)}, u32[]{:S(2)}) copy-start(bf16[128,4096]{1,0:T(8,128)(2,1)} %kernels_hbm.1) | copy-start | bytes 3145732
  4.2 0.7 %copy-start.2 = (s32[1,1,3072]{2,1,0:T(1,128)S(1)}, s32[1,1,3072]{2,1,0:T(1,128)}, u32[]{:S(2)}) copy-start(s32[1,1,3072]{2,1,0:T(1,128)} %param.16) | copy-start | bytes 36868
  4.9 0.7 %copy-start.3 = (s32[1,1,3072]{2,1,0:T(1,128)S(1)}, s32[1,1,3072]{2,1,0:T(1,128)}, u32[]{:S(2)}) copy-start(s32[1,1,3072]{2,1,0:T(1,128)} %param.17) | copy-start | bytes 36868
  5.6 0.7 %copy-start.4 = (f32[1,1,3072]{2,1,0:T(1,128)S(1)}, f32[1,1,3072]{2,1,0:T(1,128)}, u32[]{:S(2)}) copy-start(f32[1,1,3072]{2,1,0:T(1,128)} %param.18) | copy-start | bytes 36868
  6.3 0.7 %copy-start.5 = (f32[1,1,3072]{2,1,0:T(1,128)S(1)}, f32[1,1,3072]{2,1,0:T(1,128)}, u32[]{:S(2)}) copy-start(f32[1,1,3072]{2,1,0:T(1,128)} %param.19) | copy-start | bytes 36868
  7.0 0.7 %copy-start.6 = (f32[16]{0:T(128)S(1)}, f32[16]{0:T(128)}, u32[]{:S(2)}) copy-start(f32[16]{0:T(128)} %kw_ref.1) | copy-start | bytes 196
  7.7 0.7 %copy-start.7 = (f32[128]{0:T(128)S(1)}, f32[128]{0:T(128)}, u32[]{:S(2)}) copy-start(f32[128]{0:T(128)} %param.14) | copy-start | bytes 1540
  8.3 0.7 %copy-start.8 = (s32[1,1,84]{2,1,0:T(1,128)S(1)}, s32[1,1,84]{2,1,0:T(1,128)}, u32[]{:S(2)}) copy-start(s32[1,1,84]{2,1,0:T(1,128)} %param.15) | copy-start | bytes 1012

commit v2 on v1

--- a/solution.py
+++ b/solution.py
@@ -9,11 +9,12 @@
 
 BS = 128
 SEG = 1536
-ROWS = 16
 MESH = pl.DeviceIdType.MESH
 SIDES = ((0, 0), (-1, 0), (1, 0), (0, -1), (0, 1))
-OPPOSITE = (0, 2, 1, 4, 3)
-ITERS = 3
+SUMS = 3
+TURNS = 2 + 1
+UNROLL = 6
+DAMPING = 1.0
 
 
 def split_3(value):
@@ -30,11 +31,14 @@
     return high, low
 
 
-def select_3(chooser, value):
-    parts = split_3(value)
-    total = jnp.dot(chooser, parts[2], preferred_element_type=jnp.float32)
-    total = total + jnp.dot(chooser, parts[1], preferred_element_type=jnp.float32)
-    return total + jnp.dot(chooser, parts[0], preferred_element_type=jnp.float32)
+def routes(n_tx, n_ty):
+    found = {}
+    for t, (ax, ay) in enumerate(SIDES):
+        for u, (bx, by) in enumerate(SIDES):
+            offset = (ax - bx, ay - by)
+            if offset != (0, 0) and abs(offset[0]) < n_tx and abs(offset[1]) < n_ty:
+                found.setdefault(offset, []).append((t, u))
+    return sorted(found.items())
 
 
 def kernel(
@@ -42,6 +46,20 @@
     n_ty,
     raster_hbm,
     kernels_hbm,
+    kw_hbm,
+    cw_hbm,
+    need_hbm,
+    slot_hbm,
+    row_hbm,
+    level_hbm,
+    weight_hbm,
+    ids_hbm,
+    jac_hbm,
+    epe_ref,
+    step_ref,
+    raster_v,
+    kernels_v,
+    jac_v,
     kw_ref,
     cw_ref,
     need_ref,
@@ -50,12 +68,7 @@
     level_ref,
     weight_ref,
     ids_ref,
-    jac_hbm,
-    epe_ref,
-    step_ref,
-    raster_v,
-    kernels_v,
-    jac_v,
+    ids_s,
     q_own,
     edge_x,
     edge_y,
@@ -65,8 +78,8 @@
     need_pad,
     choose,
     vec,
-    gathered,
     contrib,
+    energy,
     w_cols,
     u_cols,
     w_pad,
@@ -86,7 +99,7 @@
 ):
     n_dev = n_tx * n_ty
     gx, gy = raster_hbm.shape[0], raster_hbm.shape[1]
-    pt_blocks = slot_ref.shape[1] // BS
+    pt_blocks = ids_ref.shape[0]
     nnz = ids_ref.shape[1]
     seg_blocks = step_ref.shape[1] // BS
     n_kern = kw_ref.shape[0]
@@ -98,8 +111,28 @@
     copy_k = pltpu.make_async_copy(kernels_hbm, kernels_v, local_sem.at[0])
     copy_r = pltpu.make_async_copy(raster_hbm, raster_v, local_sem.at[1])
     copy_j = pltpu.make_async_copy(jac_hbm, jac_v, local_sem.at[2])
+    small = [
+        pltpu.make_async_copy(source, target, local_sem.at[3 + i])
+        for i, (source, target) in enumerate(
+            (
+                (kw_hbm, kw_ref),
+                (cw_hbm, cw_ref),
+                (need_hbm, need_ref),
+                (slot_hbm, slot_ref),
+                (row_hbm, row_ref),
+                (level_hbm, level_ref),
+                (weight_hbm, weight_ref),
+                (ids_hbm, ids_ref),
+                (ids_hbm, ids_s),
+            )
+        )
+    ]
+    small[0].start()
+    small[1].start()
     copy_k.start()
     copy_r.start()
+    for copy in small[2:]:
+        copy.start()
     copy_j.start()
 
     def present(dx, dy):
@@ -117,6 +150,7 @@
     halo_x[...] = jnp.zeros_like(halo_x)
     halo_y[...] = jnp.zeros_like(halo_y)
     arrived[...] = jnp.zeros_like(arrived)
+    ways = routes(n_tx, n_ty)
 
     barrier = pltpu.get_barrier_semaphore()
 
@@ -128,6 +162,8 @@
     def _(offset):
         pl.semaphore_signal(barrier, inc=1, device_id=other(offset)[1], device_id_type=MESH)
 
+    small[0].wait()
+    small[1].wait()
     copy_k.wait()
     cut = cw_ref[...]
     both = jnp.zeros((2 * BS, BS), jnp.float32)
@@ -207,6 +243,8 @@
     for a in range(gx):
         start = (a + 1) * span_y + 1
         q_ext[start : start + gy, :] = q_own[a]
+    for copy in small[2:]:
+        copy.wait()
     need_pad[...] = jnp.full(need_pad.shape, -1, jnp.int32)
     need_pad[:, :need] = need_ref[...]
     listed = (lax.broadcasted_iota(jnp.int32, (BS, BS), 0) == need_pad[...]).astype(jnp.float32).astype(
@@ -214,14 +252,12 @@
     )
     choose[...] = jnp.zeros_like(choose)
     ids = ids_ref[...]
-    for t in range(1, 5):
-        ids = ids + jnp.where(ids_ref[...] >= t * seg_blocks, ROWS - seg_blocks, 0)
     for k in range(nnz):
         choose[k * pt_blocks : (k + 1) * pt_blocks, :] = (
             lax.broadcasted_iota(jnp.int32, (pt_blocks, BS), 1) == ids[:, k : k + 1]
         ).astype(jnp.float32)
-    pick = choose[...].astype(jnp.bfloat16)
-    pick_t = choose[...].T.astype(jnp.bfloat16)
+    pick_t = choose[...].T[: vec.shape[0]].astype(jnp.bfloat16)
+    pick_t = jnp.concatenate([pick_t] * 3, axis=1)
     contrib[...] = jnp.zeros_like(contrib)
     vec[...] = jnp.zeros_like(vec)
     w_pad[...] = jnp.zeros_like(w_pad)
@@ -291,169 +327,159 @@
 
     copy_j.wait()
 
-    def part_copy(turn, t, t_here):
+    def way_copy(turn, way, flip):
+        dx, dy = ways[way][0]
+        sign = -1 if flip else 1
         return pltpu.make_async_remote_copy(
-            src_ref=sent.at[turn, t],
-            dst_ref=arrived.at[turn, t_here],
-            send_sem=ex_send.at[turn, t],
-            recv_sem=ex_recv.at[turn, t_here],
-            device_id={"tx": tx + SIDES[t][0], "ty": ty + SIDES[t][1]},
+            src_ref=sent.at[turn, way],
+            dst_ref=arrived.at[turn, way],
+            send_sem=ex_send.at[turn, way],
+            recv_sem=ex_recv.at[turn, way],
+            device_id={"tx": tx + sign * dx, "ty": ty + sign * dy},
             device_id_type=MESH,
         )
 
-    def exchange(turn, parts):
-        for t in range(1, 5):
-            sent[turn, t] = parts[t]
-        for t in range(1, 5):
-
-            @pl.when(present(*SIDES[t]))
+    def start_terms(turn):
+        summed = jnp.dot(
+            pick_t,
+            jnp.concatenate(split_3(contrib[...]), axis=0),
+            preferred_element_type=jnp.float32,
+        )
+        parts = [summed[t * seg_blocks : (t + 1) * seg_blocks] for t in range(5)]
+        for way, (offset, pairs) in enumerate(ways):
+            for i, (t, u) in enumerate(pairs):
+                sent[turn, way, i * seg_blocks : (i + 1) * seg_blocks, :] = parts[t]
+
+            @pl.when(present(*offset))
             def _():
-                part_copy(turn, t, OPPOSITE[t]).start()
-
-    def receive(turn):
-        for t in range(1, 5):
-
-            @pl.when(present(*SIDES[t]))
+                way_copy(turn, way, False).start()
+
+        return parts
+
+    def end_terms(turn, parts):
+        for way, ((dx, dy), pairs) in enumerate(ways):
+
+            @pl.when(present(-dx, -dy))
             def _():
-                part_copy(turn, t, t).wait_recv()
-
-        return [arrived[turn, t] for t in range(1, 5)]
-
-    def finish(turn):
-        summed = select_3(pick_t, contrib[...])
-        parts = [summed[t * ROWS : (t + 1) * ROWS] for t in range(5)]
-        exchange(turn, parts)
-        others = receive(turn)
-        return parts[0] + (others[0] + others[1]) + (others[2] + others[3])
-
-    @pl.loop(0, pt_blocks)
+                way_copy(turn, way, True).wait_recv()
+
+        total = list(parts)
+        for way, (offset, pairs) in enumerate(ways):
+            for i, (t, u) in enumerate(pairs):
+                total[u] = total[u] + arrived[turn, way, i * seg_blocks : (i + 1) * seg_blocks, :]
+        for u in range(1, 5):
+            total[u] = jnp.where(present(*SIDES[u]), total[u], 0.0)
+        return total
+
+    def segments(u):
+        return slice(u * seg_blocks, (u + 1) * seg_blocks)
+
+    def products(values, backward):
+        for u in range(5):
+            vec[segments(u), :] = values[u]
+        energy[...] = jnp.zeros_like(energy)
+
+        @pl.loop(0, pt_blocks, unroll=UNROLL)
+        def _(n):
+            total = jac_v[n, 0] * vec[pl.ds(ids_s[n, 0], 1), :]
+            for k in range(1, nnz):
+                total = total + jac_v[n, k] * vec[pl.ds(ids_s[n, k], 1), :]
+            error = jnp.sum(total, axis=1, keepdims=True)
+            scaled = error * w_cols[n]
+            energy[...] += jnp.sum((scaled * error).reshape(BS // 8, 8, BS), axis=0)
+            if backward:
+                for k in range(nnz):
+                    contrib[pl.ds(k * pt_blocks + n, 1), :] = jnp.sum(
+                        jac_v[n, k] * scaled, axis=0, keepdims=True
+                    )
+
+    def sum_copy(turn, offset, slot):
+        peer, where = other(offset)
+        at = rank if slot is None else peer
+        return pltpu.make_async_remote_copy(
+            src_ref=part_sums.at[turn],
+            dst_ref=all_sums.at[turn, at],
+            send_sem=sum_send.at[turn, offset],
+            recv_sem=sum_recv.at[turn, at],
+            device_id=where,
+            device_id_type=MESH,
+        )
+
+    def start_sums(turn, own):
+        square = jnp.sum(own * own, axis=0, keepdims=True)
+        cross = jnp.sum(energy[...], axis=0, keepdims=True) * (1.0 / BS) + DAMPING * square
+        both = jnp.concatenate([square, cross], axis=0)
+        part_sums[turn] = both
+        all_sums[turn, rank] = both
+
+        @pl.loop(1, n_dev, unroll=3)
+        def _(offset):
+            sum_copy(turn, offset, None).start()
+
+    def end_sums(turn):
+        @pl.loop(1, n_dev, unroll=3)
+        def _(offset):
+            sum_copy(turn, offset, "theirs").wait_recv()
+
+        total = jnp.sum(jnp.sum(all_sums[turn], axis=0), axis=1, keepdims=True)
+        return total[0:1], total[1:2]
+
+    @pl.loop(0, pt_blocks, unroll=UNROLL)
     def _(n):
         for k in range(nnz):
             contrib[pl.ds(k * pt_blocks + n, 1), :] = jnp.sum(
                 jac_v[n, k] * u_cols[n], axis=0, keepdims=True
             )
 
-    def spread(own, others):
-        vec[0:ROWS, :] = own
-        for t in range(1, 5):
-            vec[t * ROWS : (t + 1) * ROWS, :] = others[t - 1]
-
-    def apply_normal(turn, own):
-        gathered[...] = select_3(pick, vec[...])
-
-        @pl.loop(0, pt_blocks)
-        def _(n):
-            total = jac_v[n, 0] * gathered[pl.ds(n, 1), :]
-            for k in range(1, nnz):
-                total = total + jac_v[n, k] * gathered[pl.ds(k * pt_blocks + n, 1), :]
-            scaled = jnp.sum(total, axis=1, keepdims=True) * w_cols[n]
-            for k in range(nnz):
-                contrib[pl.ds(k * pt_blocks + n, 1), :] = jnp.sum(
-                    jac_v[n, k] * scaled, axis=0, keepdims=True
-                )
-
-        return finish(turn) + own
-
-    def sum_copy(turn, offset):
-        peer, where = other(offset)
-        return pltpu.make_async_remote_copy(
-            src_ref=part_sums.at[turn],
-            dst_ref=all_sums.at[turn, rank],
-            send_sem=sum_send.at[turn, offset],
-            recv_sem=sum_recv.at[turn, rank],
-            device_id=where,
-            device_id_type=MESH,
-        )
-
-    def start_sums(turn, residual, image):
-        both = jnp.concatenate(
-            [
-                jnp.sum(residual * residual, axis=0, keepdims=True),
-                jnp.sum(residual * image, axis=0, keepdims=True),
-            ],
-            axis=0,
-        )
-        part_sums[turn] = both
-        all_sums[turn, rank] = both
-
-        @pl.loop(1, n_dev)
-        def _(offset):
-            sum_copy(turn, offset).start()
-
-    def end_sums(turn):
-        @pl.loop(1, n_dev)
-        def _(offset):
-            peer, where = other(offset)
-            pltpu.make_async_remote_copy(
-                src_ref=part_sums.at[turn],
-                dst_ref=all_sums.at[turn, peer],
-                send_sem=sum_send.at[turn, offset],
-                recv_sem=sum_recv.at[turn, peer],
-                device_id=where,
-                device_id_type=MESH,
-            ).wait_recv()
-
-        total = jnp.sum(jnp.sum(all_sums[turn], axis=0), axis=1, keepdims=True)
-        return total[0:1], total[1:2]
-
-    residual = -finish(0)
-    exchange(1, [residual] * 5)
-    spread(residual, receive(1))
-    image = apply_normal(2, residual)
-    start_sums(0, residual, image)
-    exchange(3, [image] * 5)
-    image_others = receive(3)
-    spread(image, image_others)
-    second = apply_normal(4, image)
-    exchange(5, [second] * 5)
-
-    norm_now, product = end_sums(0)
-    alpha = norm_now / product
-    direction, along, beyond = residual, image, second
-    step = alpha * direction
-    residual = residual - alpha * along
-    image = image - alpha * beyond
-    start_sums(1, residual, image)
-    second_others = receive(5)
-    spread(image, [w - alpha * z for w, z in zip(image_others, second_others)])
-    second = apply_normal(6, image)
-
-    norm_next, product = end_sums(1)
-    ratio = norm_next / norm_now
-    alpha = norm_next / (product - ratio * norm_next / alpha)
-    norm_now = norm_next
-    direction = residual + ratio * direction
-    along = image + ratio * along
-    beyond = second + ratio * beyond
-    step = step + alpha * direction
-    residual = residual - alpha * along
-    image = image - alpha * beyond
-    start_sums(2, residual, image)
-
-    for (dx, dy), copy in halo_copies:
-
-        @pl.when(present(dx, dy))
-        def _():
-            copy.wait_send()
-
-    for turn in range(7):
-        for t in range(1, 5):
-
-            @pl.when(present(*SIDES[t]))
-            def _():
-                part_copy(turn, t, OPPOSITE[t]).wait_send()
-
-    for turn in range(3):
-
-        @pl.loop(1, n_dev)
-        def _(offset):
-            sum_copy(turn, offset).wait_send()
-
-    norm_next, product = end_sums(2)
-    ratio = norm_next / norm_now
-    alpha = norm_next / (product - ratio * norm_next / alpha)
-    direction = residual + ratio * direction
-    step = step + alpha * direction
+    residual = [-part for part in end_terms(0, start_terms(0))]
+    direction = along = step = norm_now = alpha = None
+    for turn in range(SUMS):
+        last = turn + 1 == SUMS
+        products(residual, not last)
+        if not last:
+            parts = start_terms(turn + 1)
+        start_sums(turn, residual[0])
+        if last:
+            for (dx, dy), copy in halo_copies:
+
+                @pl.when(present(dx, dy))
+                def _():
+                    copy.wait_send()
+
+            for before in range(TURNS):
+                for way, (offset, pairs) in enumerate(ways):
+
+                    @pl.when(present(*offset))
+                    def _():
+                        way_copy(before, way, False).wait_send()
+
+            for before in range(SUMS):
+
+                @pl.loop(1, n_dev, unroll=3)
+                def _(offset):
+                    sum_copy(before, offset, None).wait_send()
+
+        else:
+            image = [
+                part + DAMPING * value
+                for part, value in zip(end_terms(turn + 1, parts), residual)
+            ]
+        norm_next, product = end_sums(turn)
+        if turn == 0:
+            alpha = norm_next / product
+            direction, step = residual[0], alpha * residual[0]
+            along = image
+        else:
+            ratio = norm_next / norm_now
+            alpha = norm_next / (product - ratio * norm_next / alpha)
+            direction = residual[0] + ratio * direction
+            step = step + alpha * direction
+            if not last:
+                along = [new + ratio * old for new, old in zip(image, along)]
+        norm_now = norm_next
+        if not last:
+            residual = [value - alpha * change for value, change in zip(residual, along)]
+
     for j in range(seg_blocks):
         step_ref[:, j * BS : (j + 1) * BS] = step[j : j + 1, :]
 
@@ -477,11 +503,12 @@
     pt_blocks, nnz = jac_ids.shape[-2:]
     gx, gy = raster.shape[:2]
     segments = SEG
+    wide = 2 * (SEG // BS)
+    n_ways = len(routes(n_tx, n_ty))
     n_dev = n_tx * n_ty
     f32 = jnp.float32
     vmem = pl.BlockSpec(memory_space=pltpu.VMEM)
     anywhere = pl.BlockSpec(memory_space=pl.ANY)
-    smem = pl.BlockSpec(memory_space=pltpu.SMEM)
     dma = pltpu.SemaphoreType.DMA
     epe, step = pl.pallas_call(
         functools.partial(kernel, n_tx, n_ty),
@@ -489,12 +516,21 @@
             jax.ShapeDtypeStruct((1, points), f32),
             jax.ShapeDtypeStruct((1, segments), f32),
         ),
-        in_specs=[anywhere, anywhere, smem] + [vmem] * 7 + [anywhere],
+        in_specs=[anywhere] * 11,
         out_specs=(vmem, vmem),
         scratch_shapes=[
             pltpu.VMEM(raster.shape, jnp.bfloat16),
             pltpu.VMEM(kernels.shape, jnp.bfloat16),
             pltpu.VMEM((pt_blocks, nnz, BS, BS), f32),
+            pltpu.SMEM(kernel_weights.shape, f32),
+            pltpu.VMEM((1, BS), f32),
+            pltpu.VMEM((1, need_list.shape[-1]), jnp.int32),
+            pltpu.VMEM((1, points), jnp.int32),
+            pltpu.VMEM((1, points), jnp.int32),
+            pltpu.VMEM((1, points), f32),
+            pltpu.VMEM((1, points), f32),
+            pltpu.VMEM((pt_blocks, nnz), jnp.int32),
+            pltpu.SMEM((pt_blocks, nnz), jnp.int32),
             pltpu.VMEM((gx, gy, BS), f32),
             pltpu.VMEM((2, gy, BS), f32),
             pltpu.VMEM((2, gx, BS), f32),
@@ -503,28 +539,28 @@
             pltpu.VMEM((BS, BS), f32),
             pltpu.VMEM((1, BS), jnp.int32),
             pltpu.VMEM((BS, BS), f32),
+            pltpu.VMEM((64, BS), f32),
             pltpu.VMEM((BS, BS), f32),
-            pltpu.VMEM((BS, BS), f32),
-            pltpu.VMEM((BS, BS), f32),
+            pltpu.VMEM((8, BS), f32),
             pltpu.VMEM((pt_blocks, BS, BS), f32),
             pltpu.VMEM((pt_blocks, BS, BS), f32),
             pltpu.VMEM((BS, BS), f32),
-            pltpu.VMEM((7, 5, ROWS, BS), f32),
-            pltpu.VMEM((7, 5, ROWS, BS), f32),
-            pltpu.VMEM((3, 2, BS), f32),
-            pltpu.VMEM((3, n_dev, 2, BS), f32),
-            dma((3,)),
+            pltpu.VMEM((TURNS, n_ways, wide, BS), f32),
+            pltpu.VMEM((TURNS, n_ways, wide, BS), f32),
+            pltpu.VMEM((SUMS, 2, BS), f32),
+            pltpu.VMEM((SUMS, n_dev, 2, BS), f32),
+            dma((12,)),
             dma((2, 3)),
             dma((2, 3)),
             dma((2,)),
             dma((2,)),
-            dma((7, 5)),
-            dma((7, 5)),
-            dma((3, n_dev)),
-            dma((3, n_dev)),
+            dma((TURNS, n_ways)),
+            dma((TURNS, n_ways)),
+            dma((SUMS, n_dev)),
+            dma((SUMS, n_dev)),
         ],
         compiler_params=pltpu.CompilerParams(
-            collective_id=0, has_side_effects=True, vmem_limit_bytes=48 * 1024 * 1024
+            collective_id=0, has_side_effects=True, vmem_limit_bytes=56 * 1024 * 1024
         ),
     )(
         raster,

time: 61.5 us -> 39.9 us (0.65)
  Pallas kernels: 50.8 us -> 35 us
  local copies, waits for them, and re-layouts: 9.56 us -> 3.95 us
    pallas_call x1, Pallas kernels: 50.8 us -> 35 us  [on_device(): pl.pallas_call(functools.partial(kernel, n_tx, n_ty), out_shape=(jax.Shap...]
    unnamed x20 -> x2, local copies, waits for them, and re-layouts: 8.8 us -> 2.59 us
where the time goes in v2:
time: 39.9 us; the launch traced here: 39.6 us
  Pallas kernels  35 us (88%)
  local copies, waits for them, and re-layouts  3.95 us (10%)
  between operations  0.64 us (2%)
    pallas_call x1, Pallas kernels, on_device(): pl.pallas_call(functools.partial(kernel, n_tx, n_ty), out_shape=(jax.Shap...  35 us
    unnamed x2, local copies, waits for them, and re-layouts  2.59 us
    reshape x1, local copies, waits for them, and re-layouts, on_device(): jac_ids.reshape(pt_blocks, nnz)  1.36 us

profile of v2, /device:TPU:0, one launch (start us, length us, event | category | flops | bytes accessed | tf_op | source)
XLA Modules:
  0.0 39.6 jit_solution(9313615931459325018)
XLA Ops:
  0.6 1.4 %copy.13.ids_hbm = s32[24,4]{1,0:T(8,128)} copy(s32[24,4]{0,1:T(4,128)} %bitcast.17) | data formatting | bytes 768 | tf_op jit(solution)/shard_map/reshape | solution.py:575
  2.0 35.0 %shard_map.122 = (f32[1,3072]{1,0:T(1,128)}, f32[1,1536]{1,0:T(1,128)}) custom-call(bf16[8,8,128,128]{3,2,1,0:T(8,128)(2,1)} %raster_hbm.1, bf16[128,4096]{1,0:T(8,128)(2,1)} %kernels_hbm.1, f32[16]{0:T(128)} %kw_hbm.1, f32[1,128]{1,0:T(1,128)} %bitcast.18, s32[1,84]{1,0:T(1,128)} %bitcast.19, s32[1,3072]{1,0:T(1,128)} %bitcast.12, s32[1,3072]{1,0:T(1,128)} %bitcast.13, ...), custom_call_target="tpu_custom_call" | custom-call | tf_op jit(solution)/shard_map/pallas_call | solution.py:513
  37.0 1.3 %copy.16 = f32[1,1,3072]{2,1,0:T(1,128)} copy(f32[1,1,3072]{2,1,0:T(1,128)} %bitcast.11) | data formatting | bytes 24576
  38.3 1.3 %copy.17 = f32[1,1,1536]{2,1,0:T(1,128)} copy(f32[1,1,1536]{2,1,0:T(1,128)} %bitcast.16) | data formatting | bytes 12288

commit v3 on v2

--- a/solution.py
+++ b/solution.py
@@ -99,8 +99,9 @@
 ):
     n_dev = n_tx * n_ty
     gx, gy = raster_hbm.shape[0], raster_hbm.shape[1]
-    pt_blocks = ids_ref.shape[0]
-    nnz = ids_ref.shape[1]
+    pt_blocks = ids_ref.shape[1]
+    nnz = ids_ref.shape[0]
+    stride = BS // nnz
     seg_blocks = step_ref.shape[1] // BS
     n_kern = kw_ref.shape[0]
     span_y = gy + 2
@@ -187,7 +188,7 @@
         jnp.int32, (1, BS, BS), 2
     )
 
-    @pl.loop(0, gx)
+    @pl.loop(0, gx, unroll=4)
     def _(a):
         rows = raster_v[a].reshape(gy * BS, BS)
         product = jnp.dot(rows, form, preferred_element_type=jnp.float32)
@@ -251,12 +252,11 @@
         jnp.bfloat16
     )
     choose[...] = jnp.zeros_like(choose)
-    ids = ids_ref[...]
     for k in range(nnz):
-        choose[k * pt_blocks : (k + 1) * pt_blocks, :] = (
-            lax.broadcasted_iota(jnp.int32, (pt_blocks, BS), 1) == ids[:, k : k + 1]
+        choose[:, k * stride : k * stride + pt_blocks] = (
+            lax.broadcasted_iota(jnp.int32, (choose.shape[0], pt_blocks), 0) == ids_ref[k : k + 1, :]
         ).astype(jnp.float32)
-    pick_t = choose[...].T[: vec.shape[0]].astype(jnp.bfloat16)
+    pick_t = choose[...].astype(jnp.bfloat16)
     pick_t = jnp.concatenate([pick_t] * 3, axis=1)
     contrib[...] = jnp.zeros_like(contrib)
     vec[...] = jnp.zeros_like(vec)
@@ -374,24 +374,28 @@
     def segments(u):
         return slice(u * seg_blocks, (u + 1) * seg_blocks)
 
-    def products(values, backward):
+    def forward(values):
         for u in range(5):
             vec[segments(u), :] = values[u]
         energy[...] = jnp.zeros_like(energy)
 
         @pl.loop(0, pt_blocks, unroll=UNROLL)
         def _(n):
-            total = jac_v[n, 0] * vec[pl.ds(ids_s[n, 0], 1), :]
+            total = jac_v[n, 0] * vec[pl.ds(ids_s[0, n], 1), :]
             for k in range(1, nnz):
-                total = total + jac_v[n, k] * vec[pl.ds(ids_s[n, k], 1), :]
+                total = total + jac_v[n, k] * vec[pl.ds(ids_s[k, n], 1), :]
             error = jnp.sum(total, axis=1, keepdims=True)
             scaled = error * w_cols[n]
+            u_cols[n] = scaled
             energy[...] += jnp.sum((scaled * error).reshape(BS // 8, 8, BS), axis=0)
-            if backward:
-                for k in range(nnz):
-                    contrib[pl.ds(k * pt_blocks + n, 1), :] = jnp.sum(
-                        jac_v[n, k] * scaled, axis=0, keepdims=True
-                    )
+
+    def backward():
+        @pl.loop(0, pt_blocks, unroll=UNROLL)
+        def _(n):
+            for k in range(nnz):
+                contrib[pl.ds(k * stride + n, 1), :] = jnp.sum(
+                    jac_v[n, k] * u_cols[n], axis=0, keepdims=True
+                )
 
     def sum_copy(turn, offset, slot):
         peer, where = other(offset)
@@ -412,33 +416,28 @@
         part_sums[turn] = both
         all_sums[turn, rank] = both
 
-        @pl.loop(1, n_dev, unroll=3)
+        @pl.loop(1, n_dev, unroll=5)
         def _(offset):
             sum_copy(turn, offset, None).start()
 
     def end_sums(turn):
-        @pl.loop(1, n_dev, unroll=3)
+        @pl.loop(1, n_dev, unroll=5)
         def _(offset):
             sum_copy(turn, offset, "theirs").wait_recv()
 
         total = jnp.sum(jnp.sum(all_sums[turn], axis=0), axis=1, keepdims=True)
         return total[0:1], total[1:2]
 
-    @pl.loop(0, pt_blocks, unroll=UNROLL)
-    def _(n):
-        for k in range(nnz):
-            contrib[pl.ds(k * pt_blocks + n, 1), :] = jnp.sum(
-                jac_v[n, k] * u_cols[n], axis=0, keepdims=True
-            )
-
+    backward()
     residual = [-part for part in end_terms(0, start_terms(0))]
     direction = along = step = norm_now = alpha = None
     for turn in range(SUMS):
         last = turn + 1 == SUMS
-        products(residual, not last)
+        forward(residual)
+        start_sums(turn, residual[0])
         if not last:
+            backward()
             parts = start_terms(turn + 1)
-        start_sums(turn, residual[0])
         if last:
             for (dx, dy), copy in halo_copies:
 
@@ -455,7 +454,7 @@
 
             for before in range(SUMS):
 
-                @pl.loop(1, n_dev, unroll=3)
+                @pl.loop(1, n_dev, unroll=5)
                 def _(offset):
                     sum_copy(before, offset, None).wait_send()
 
@@ -482,6 +481,17 @@
 
     for j in range(seg_blocks):
         step_ref[:, j * BS : (j + 1) * BS] = step[j : j + 1, :]
+
+
+def deliver(epe_v, step_v, epe_hbm, step_hbm, sem):
+    copies = [
+        pltpu.make_async_copy(epe_v, epe_hbm, sem.at[0]),
+        pltpu.make_async_copy(step_v, step_hbm, sem.at[1]),
+    ]
+    for copy in copies:
+        copy.start()
+    for copy in copies:
+        copy.wait()
 
 
 def on_device(
@@ -529,8 +539,8 @@
             pltpu.VMEM((1, points), jnp.int32),
             pltpu.VMEM((1, points), f32),
             pltpu.VMEM((1, points), f32),
-            pltpu.VMEM((pt_blocks, nnz), jnp.int32),
-            pltpu.SMEM((pt_blocks, nnz), jnp.int32),
+            pltpu.VMEM((nnz, pt_blocks), jnp.int32),
+            pltpu.SMEM((nnz, pt_blocks), jnp.int32),
             pltpu.VMEM((gx, gy, BS), f32),
             pltpu.VMEM((2, gy, BS), f32),
             pltpu.VMEM((2, gx, BS), f32),
@@ -538,7 +548,7 @@
             pltpu.VMEM((2, gx, BS), f32),
             pltpu.VMEM((BS, BS), f32),
             pltpu.VMEM((1, BS), jnp.int32),
-            pltpu.VMEM((BS, BS), f32),
+            pltpu.VMEM((64, BS), f32),
             pltpu.VMEM((64, BS), f32),
             pltpu.VMEM((BS, BS), f32),
             pltpu.VMEM((8, BS), f32),
@@ -572,9 +582,19 @@
         point_row.reshape(1, points),
         threshold.reshape(1, points),
         point_weight.reshape(1, points),
-        jac_ids.reshape(pt_blocks, nnz),
+        jac_ids.reshape(pt_blocks, nnz).T,
         jacobian.reshape(pt_blocks, nnz, BS, BS),
     )
+    epe, step = pl.pallas_call(
+        deliver,
+        out_shape=(
+            jax.ShapeDtypeStruct((1, points), f32),
+            jax.ShapeDtypeStruct((1, segments), f32),
+        ),
+        in_specs=[vmem, vmem],
+        out_specs=(anywhere, anywhere),
+        scratch_shapes=[dma((2,))],
+    )(epe, step)
     return epe.reshape(1, 1, points), step.reshape(1, 1, segments)
 
 

time: 39.9 us -> 35 us (0.88)
  local copies, waits for them, and re-layouts: 3.95 us -> 0 us
  Pallas kernels: 35 us -> 34.1 us
    unnamed x2 -> x0, local copies, waits for them, and re-layouts: 2.59 us -> none
    pallas_call x1, Pallas kernels: 35 us -> 32.8 us  [on_device(): pl.pallas_call(functools.partial(kernel, n_tx, n_ty), out_shape=(jax.Shap...]
    reshape x1 -> x0, local copies, waits for them, and re-layouts: 1.36 us -> none  [on_device(): jac_ids.reshape(pt_blocks, nnz)]
    pallas_call x0 -> x1, Pallas kernels: none -> 1.33 us  [on_device(): pl.pallas_call(deliver, out_shape=(jax.ShapeDtypeStruct((1, points), f32)...]
where the time goes in v3:
time: 35 us; the launch traced here: 34.7 us
  Pallas kernels  34.1 us (97%)
  between operations  0.64 us (2%)
    pallas_call x1, Pallas kernels, on_device(): pl.pallas_call(functools.partial(kernel, n_tx, n_ty), out_shape=(jax.Shap...  32.8 us
    pallas_call x1, Pallas kernels, on_device(): pl.pallas_call(deliver, out_shape=(jax.ShapeDtypeStruct((1, points), f32)...  1.33 us

profile of v3, /device:TPU:0, one launch (start us, length us, event | category | flops | bytes accessed | tf_op | source)
XLA Modules:
  0.0 34.7 jit_solution(17717664688584052542)
XLA Ops:
  0.6 32.8 %shard_map.122 = (f32[1,3072]{1,0:T(1,128)}, f32[1,1536]{1,0:T(1,128)}) custom-call(bf16[8,8,128,128]{3,2,1,0:T(8,128)(2,1)} %raster_hbm.1, bf16[128,4096]{1,0:T(8,128)(2,1)} %kernels_hbm.1, f32[16]{0:T(128)} %kw_hbm.1, f32[1,128]{1,0:T(1,128)} %bitcast.18, s32[1,84]{1,0:T(1,128)} %bitcast.19, s32[1,3072]{1,0:T(1,128)} %bitcast.13, s32[1,3072]{1,0:T(1,128)} %bitcast.14, ...), custom_call_target="tpu_custom_call" | custom-call | tf_op jit(solution)/shard_map/pallas_call | solution.py:523
  33.4 1.3 %shard_map.123 = (f32[1,3072]{1,0:T(1,128)}, f32[1,1536]{1,0:T(1,128)}) custom-call(f32[1,3072]{1,0:T(1,128)} %get-tuple-element.6.epe_v, f32[1,1536]{1,0:T(1,128)} %get-tuple-element.7.step_v), custom_call_target="tpu_custom_call" | custom-call | tf_op jit(solution)/shard_map/pallas_call | solution.py:588
